TPU v7x, 256 devices: a whole 4x4x8 slice. The times are simulated.
256 devices in a mesh: dom: 16 (over z_hi, x, core), edge: 16 (over y, z_lo).
Axes of the slice: x: 4, y: 4, z: 8 (z_hi: 2, z_lo: 4; z = z_hi * 4 + z_lo), core: 2. Of those that a mesh axis runs over, the one named last changes fastest.
Arguments:
- embeddings: float32 [24576, 400], P(('dom', 'edge')), may hold values from -1.5 to 1.5
- adagrad_state: float32 [24576], P(('dom', 'edge')), may hold values from 0.001 to 0.05
- source_rows: int32 [2, 131072], P(None, ('dom', 'edge')), may hold values from 0 to 1535
- target_rows: int32 [2, 131072], P(None, ('dom', 'edge')), may hold values from 0 to 1535
- negative_rows: int32 [2, 256000], P(None, ('dom', 'edge')), may hold values from 0 to 1535
- edge_counts: int32 [2, 256], P(None, ('dom', 'edge')), may hold values from 128 to 512, as said below
Outputs:
- new_embeddings: float32 [24576, 400], P(('dom', 'edge'))
- new_state: float32 [24576], P(('dom', 'edge'))
Inputs may be any that keep to these rules, and one draw needn't show every extreme that they name: `edge_counts`: in each round every device has between 128 and 512 live edge slots, its first ones; in each round some device has all 512.
All inputs are finite; a program needn't handle non-finite values.
Results may differ from a plain program's by a relative error of at most 0.0021.
Values may be sent and summed in bfloat16 or wider, within the bound.
A program may use at most 64 MiB of HBM per device.

v0:
```python
import jax
import jax.numpy as jnp
from jax import lax
from jax.experimental import pallas as pl
from jax.experimental.pallas import tpu as pltpu
from jax.sharding import PartitionSpec as P

ROUNDS = 2
WIDTH = 400
LANES = 512
MAIN = 384
ROWS = 96
PACKED = 304
SLOTS = 512
BLOCK = 384
ENT = 1536
NEG = 1000
learning_rate = 0.1

MESH = pl.DeviceIdType.MESH
f32 = jnp.float32
bf16 = jnp.bfloat16


def flip(z, k):
    if k == 0:
        return z
    if k == 1:
        return z + 1 - 2 * (z % 2)
    if k == 2:
        return (z + 2) % 4
    return 3 - z


def pack_rest(rest):
    out = rest[0:16, :]
    for g in range(1, 6):
        out = out + pltpu.roll(rest[16 * g : 16 * g + 16, :], 16 * g, 1)
    return out


def rest_piece(rest, g):
    lane = lax.broadcasted_iota(jnp.int32, (16, 128), 1)
    piece = rest if g == 0 else pltpu.roll(rest, 128 - 16 * g, 1)
    return jnp.where(lane < 16, piece, 0.0)


def kernel(
    emb_hbm, state_hbm, source_hbm, target_hbm, negative_hbm, count_hbm, emb_out, state_out,
    emb_ref, state_ref, source_ref, target_ref, negative_ref, count_ref, idx_ref, E, G, state_col, idx_far, own_pk, Lo, Lp, To, Tp, hot, HS, cnt, MT, tmp,
    PBs, PBr, OBs, OBr, YBs, YBr, GO, ZBs, ZBr, Sv, Gv,
    ss, r_own, r_par, r_parq, r_pb, r_ob, r_yb, r_zb, r_idx, r_in,
):
    d, e = lax.axis_index("dom"), lax.axis_index("edge")
    zh, x, c = d // 8, (d // 2) % 4, d % 2
    y, z = e // 4, e % 4

    def dev(zh_, c_, y_, z_):
        return (zh_ * 8 + x * 2 + c_, y_ * 4 + z_)

    yp, ym, yo = (y + 1) % 4, (y + 3) % 4, (y + 2) % 4
    up, down, sib = dev(zh, c, yp, z), dev(zh, c, ym, z), dev(zh, 1 - c, y, z)
    mover = zh != c

    barrier = pltpu.get_barrier_semaphore()
    for to in (up, down, sib) + tuple(dev(zh, c, y, flip(z, k)) for k in (1, 2, 3)):
        pl.semaphore_signal(barrier, inc=1, device_id=to, device_id_type=MESH)

    @pl.when(mover)
    def _():
        for k in range(4):
            pl.semaphore_signal(
                barrier, inc=1, device_id=dev(c, zh, y, flip(z, k)), device_id_type=MESH
            )

    started = []
    count = [0]

    def send(src, dst, sem, to, when=None):
        slot = count[0]
        count[0] += 1

        def make():
            return pltpu.make_async_remote_copy(
                src_ref=src, dst_ref=dst, send_sem=ss.at[slot], recv_sem=sem,
                device_id=to, device_id_type=MESH,
            )

        if when is None:
            make().start()
        else:
            pl.when(when)(lambda: make().start())
        started.append((make, when))

    def drain():
        for make, when in started:
            if when is None:
                make().wait_send()
            else:
                pl.when(when)(lambda make=make: make().wait_send())
        started.clear()

    def arrived(dst, sem, when=None):
        def wait():
            pltpu.make_async_remote_copy(
                src_ref=dst, dst_ref=dst, send_sem=ss.at[0], recv_sem=sem,
                device_id=sib, device_id_type=MESH,
            ).wait_recv()

        if when is None:
            wait()
        else:
            pl.when(when)(wait)

    loads = []
    for i, (src, dst) in enumerate(
        (
            (emb_hbm, emb_ref), (state_hbm, state_ref), (source_hbm, source_ref),
            (target_hbm, target_ref), (negative_hbm, negative_ref), (count_hbm, count_ref),
        )
    ):
        loads.append(pltpu.make_async_copy(src, dst, r_in.at[i]))
        loads[-1].start()
    idx_ref[...] = jnp.full((ROUNDS, 8, SLOTS), -1, jnp.int32)
    for load in loads:
        load.wait()
    for r in range(ROUNDS):
        idx_ref[r, 0:1, :] = source_ref[r : r + 1, :]
        idx_ref[r, 1:2, :] = target_ref[r : r + 1, :]
        idx_ref[r, 2:3, :] = negative_ref[r : r + 1, :SLOTS]
        idx_ref[r, 3:4, : NEG - SLOTS] = negative_ref[r : r + 1, SLOTS:]
        idx_ref[r, 4:5, :] = jnp.broadcast_to(count_ref[:, r : r + 1], (1, SLOTS))

    E[:, MAIN:] = jnp.zeros((ROWS, LANES - MAIN), f32)
    E[:, :WIDTH] = emb_ref[...]
    diag = lax.broadcasted_iota(jnp.int32, (ROWS, ROWS), 0) == lax.broadcasted_iota(
        jnp.int32, (ROWS, ROWS), 1
    )
    state_col[...] = jnp.sum(
        jnp.where(diag, jnp.broadcast_to(state_ref[...], (ROWS, ROWS)), 0.0), axis=1, keepdims=True
    )

    def pack_own(r):
        for g in range(3):
            own_pk[r, ROWS * g : ROWS * (g + 1), :] = E[:, 128 * g : 128 * (g + 1)].astype(bf16)
        rest = E[:, MAIN:].astype(bf16).astype(f32)
        own_pk[r, 3 * ROWS :, :] = pack_rest(rest).astype(bf16)

    def row_of(r, i):
        return (idx_ref[0, i : i + 1, :] if r == 0 else idx_far[i : i + 1, :]).astype(f32)

    def source_hot(r):
        column = jnp.transpose(jnp.broadcast_to(row_of(r, 0), (128, SLOTS)))
        lane = lax.broadcasted_iota(jnp.int32, (SLOTS, 128), 1)
        for b, block in enumerate((y, yp, ym, yo)):
            for t in range(3):
                at = (lane + (block * BLOCK + 128 * t)).astype(f32)
                hot[b, :, 128 * t : 128 * (t + 1)] = jnp.where(column == at, 1.0, 0.0).astype(bf16)

    def scatter_hot(r):
        source = row_of(r, 0)
        row = lax.broadcasted_iota(jnp.int32, (128, SLOTS), 0)

        @pl.loop(0, ENT // 128)
        def _(i):
            at = (row + i * 128).astype(f32)
            HS[pl.ds(i * 128, 128), :] = jnp.where(source == at, 1.0, 0.0).astype(bf16)

    def multiplicity(r):
        first, second = row_of(r, 2), row_of(r, 3)
        row = lax.broadcasted_iota(jnp.int32, (128, SLOTS), 0)

        @pl.loop(0, ENT // 128)
        def _(i):
            at = (row + i * 128).astype(f32)
            total = jnp.where(first == at, 1.0, 0.0) + jnp.where(second == at, 1.0, 0.0)
            cnt[pl.ds(i * 128, 128), :] = jnp.sum(total, axis=1, keepdims=True) * (1.0 / NEG)

    def assemble(L, T, r, slot):
        base = slot * ROWS
        for g in range(3):
            T[pl.ds(base, ROWS), 128 * g : 128 * (g + 1)] = L[r, slot, ROWS * g : ROWS * (g + 1), :]
        rest = L[r, slot, 3 * ROWS :, :].astype(f32)
        for g in range(6):
            T[pl.ds(base + 16 * g, 16), MAIN:] = rest_piece(rest, g).astype(bf16)

    def pack_chunk(ref, at):
        base = at * ROWS
        pieces = [ref[pl.ds(base, ROWS), 128 * g : 128 * (g + 1)] for g in range(3)]
        return pieces + [pack_rest(ref[pl.ds(base, ROWS), MAIN:])]

    spans = [(0, ROWS), (ROWS, 2 * ROWS), (2 * ROWS, 3 * ROWS), (3 * ROWS, PACKED)]

    for r in range(ROUNDS):
        far = mover if r == 1 else None
        zt, ct = (zh, c) if r == 0 else (c, zh)
        stay = None if r == 0 else jnp.logical_not(mover)

        pack_own(r)

        def keep(r=r):
            Lo[r, e] = own_pk[r]

        if r == 0:
            keep()
            source_hot(0)
            pl.semaphore_wait(barrier, 6 + 4 * ((zh + c) % 2))
        else:
            pl.when(stay)(keep)
        def place(k, r=r):
            near = flip(z, k)
            return near if r == 0 else near + ((zh + c) % 2) * (3 - 2 * near)

        def turn(k, r=r):
            if k % 2 == 0:
                return flip(z, k)
            a, b = flip(z, k), flip(z, 4 - k)
            return a if r == 0 else a + ((zh + c) % 2) * (b - a)

        for k in range(4):
            if k > 0 or r == 1:
                send(
                    own_pk.at[r], Lo.at[r, e], r_own.at[r, e], dev(zt, ct, y, turn(k)),
                    mover if k == 0 else None,
                )

        def block_wait(block, k, to=None):
            slot = block * 4 + turn(k)
            arrived(Lo.at[r, slot], r_own.at[r, slot])
            if to is not None:
                send(Lo.at[r, slot], Lo.at[r, slot], r_own.at[r, slot], to)

        def line(k):
            slot = y * 4 + turn(k)
            if k > 0:
                arrived(Lo.at[r, slot], r_own.at[r, slot])
            elif r == 1:
                arrived(Lo.at[r, slot], r_own.at[r, slot], mover)
            send(Lo.at[r, slot], Lo.at[r, slot], r_own.at[r, slot], up)
            send(Lo.at[r, slot], Lo.at[r, slot], r_own.at[r, slot], down)

        def sibling_block(block, q):
            send(Lo.at[r, pl.ds(block * 4, 4)], Lp.at[r, pl.ds(block * 4, 4)], r_par.at[r, q], sib)

        def opposite(k):
            slot = yo * 4 + turn(k)
            arrived(Lo.at[r, slot], r_own.at[r, slot])
            send(Lo.at[r, slot], Lp.at[r, slot], r_parq.at[r, turn(k)], sib)

        def sources(b, block):
            for k in range(4):
                assemble(Lo, To, r, block * 4 + k)
            rows = To[pl.ds(pl.multiple_of(block * BLOCK, BLOCK), BLOCK), :]
            part = jnp.dot(hot[b], rows, preferred_element_type=f32)
            Sv[...] = part if b == 0 else Sv[...] + part

        def partner(q, block):
            arrived(Lp.at[r, pl.ds(block * 4, 4)], r_par.at[r, q])
            for k in range(4):
                assemble(Lp, Tp, r, block * 4 + k)

        line(0)
        if r == 0:
            send(idx_ref.at[1], idx_far, r_idx.at[0], dev(c, zh, y, z), mover)

            @pl.when(jnp.logical_not(mover))
            def _():
                idx_far[...] = idx_ref[1]

            multiplicity(0)
        else:
            arrived(idx_far, r_idx.at[0], mover)
            source_hot(1)
        line(1)
        line(2)
        line(3)
        sibling_block(y, 0)
        scatter_hot(r)
        block_wait(ym, 0, up)
        block_wait(yp, 0)
        block_wait(yp, 1, down)
        block_wait(ym, 1)
        block_wait(ym, 2, up)
        block_wait(yp, 2)
        block_wait(yp, 3, down)
        block_wait(ym, 3)
        sibling_block(ym, 1)
        sibling_block(yp, 2)
        opposite(0)
        opposite(1)
        sources(0, y)
        if r == 1:
            multiplicity(1)
        sources(1, yp)
        partner(0, y)
        sources(2, ym)
        partner(1, ym)
        opposite(2)
        opposite(3)
        partner(2, yp)
        sources(3, yo)
        for k in range(4):
            slot = yo * 4 + turn(k)
            arrived(Lp.at[r, slot], r_parq.at[r, turn(k)])
            assemble(Lp, Tp, r, slot)

        half = (Sv[...] * 0.5).astype(bf16)
        target = row_of(r, 1)
        slot_at = lax.broadcasted_iota(jnp.int32, (1, SLOTS), 1).astype(f32)
        live = jnp.where(slot_at < row_of(r, 4), 0.5, 0.0)

        def weights(i, held):
            rows = pl.ds(pl.multiple_of(i * BLOCK, BLOCK), BLOCK)
            t = jnp.tanh(
                lax.dot_general(
                    Tp[rows, :], half, (((1,), (1,)), ((), ())), preferred_element_type=f32
                )
            )
            at = (lax.broadcasted_iota(jnp.int32, (BLOCK, SLOTS), 0) + i * BLOCK).astype(f32)
            same = target == at
            m = live * (cnt[rows, :] * (1.0 + t) + jnp.where(same, t - 1.0, 0.0))
            weight = m.astype(bf16)
            MT[rows, :] = weight
            return held + jnp.sum(jnp.where(same, m, 0.0), axis=0, keepdims=True)

        held = lax.fori_loop(0, ENT // BLOCK, weights, jnp.zeros((1, SLOTS), f32))
        rounded = held.astype(bf16).astype(f32)
        ratio = jnp.where(rounded == 0.0, 1.0, held / jnp.where(rounded == 0.0, 1.0, rounded))
        ratio = jnp.transpose(jnp.broadcast_to(ratio, (128, SLOTS)))
        ratio = jnp.concatenate([ratio] * (LANES // 128), axis=1)

        scaled = (Sv[...] * ratio).astype(bf16)

        def peer(b, block):
            rows = pl.ds(pl.multiple_of(block * BLOCK, BLOCK), BLOCK)
            tmp[...] = jnp.dot(MT[rows, :], scaled, preferred_element_type=f32)
            for k in range(4):
                for (lo, hi), piece in zip(spans, pack_chunk(tmp, k)):
                    PBs[r, b, k, lo:hi, :] = piece.astype(bf16)
            send(PBs.at[r, b], PBr.at[r, b], r_pb.at[r, b], sib)

        def own(b, block):
            rows = pl.ds(pl.multiple_of(block * BLOCK, BLOCK), BLOCK)
            tmp[...] = jnp.dot(HS[rows, :], grad, preferred_element_type=f32)
            arrived(PBr.at[r, b], r_pb.at[r, b])
            for k in (3, 2, 1, 0):
                for (lo, hi), piece in zip(spans, pack_chunk(tmp, place(k))):
                    total = piece + PBr[r, b, place(k), lo:hi, :].astype(f32)
                    if b == 0:
                        OBs[r, k, lo:hi, :] = total.astype(bf16)
                    elif b < 3 and k % 2 == b % 2:
                        YBs[r, b - 1, k, lo:hi, :] = total.astype(bf16)
                    else:
                        GO[b - 1, k, lo:hi, :] = total

        def send_opposite(k):
            send(OBs.at[r, k], OBr.at[r, k], r_ob.at[r, k], up if k % 2 == 0 else down)

        def send_block(q, k):
            send(YBs.at[r, q, k], YBr.at[r, q, k], r_yb.at[r, q, k], up if q == 0 else down)

        def add_opposite(k):
            q = k % 2
            arrived(OBr.at[r, k], r_ob.at[r, k])
            YBs[r, q, k] = (GO[q, k] + OBr[r, k].astype(f32)).astype(bf16)
            send_block(q, k)

        def to_line(k):
            arrived(YBr.at[r, 0, k], r_yb.at[r, 0, k])
            arrived(YBr.at[r, 1, k], r_yb.at[r, 1, k])
            GO[2, k] = GO[2, k] + YBr[r, 0, k].astype(f32) + YBr[r, 1, k].astype(f32)
            if k > 0 or r == 1:
                ZBs[r, k] = GO[2, k].astype(bf16)
                send(
                    ZBs.at[r, k], ZBr.at[r, k], r_zb.at[r, k], dev(zt, ct, y, place(k)),
                    None if k > 0 else mover,
                )

        peer(0, yo)
        grad = lax.dot_general(
            MT[...], Tp[...], (((0,), (0,)), ((), ())), preferred_element_type=f32
        )
        grad = (grad * ratio).astype(bf16)
        own(0, yo)
        send_opposite(3)
        send_opposite(2)
        peer(1, yp)
        peer(2, ym)
        own(1, yp)
        send_block(0, 3)
        own(2, ym)
        send_block(1, 2)
        send_opposite(1)
        send_opposite(0)
        peer(3, y)
        add_opposite(2)
        add_opposite(3)
        send_block(0, 1)
        send_block(1, 0)
        own(3, y)
        to_line(3)
        to_line(2)
        add_opposite(0)
        add_opposite(1)
        to_line(1)
        to_line(0)
        if r == ROUNDS - 1:
            drain()
        if r == 1:
            arrived(ZBr.at[r, 0], r_zb.at[r, 0], mover)

            @pl.when(mover)
            def _():
                GO[2, 0] = ZBr[1, 0].astype(f32)

        total = GO[2, 0]
        for k in (1, 2, 3):
            arrived(ZBr.at[r, k], r_zb.at[r, k])
            total = total + ZBr[r, k].astype(f32)

        for g in range(3):
            G[:, 128 * g : 128 * (g + 1)] = total[ROWS * g : ROWS * (g + 1), :]
        for g in range(6):
            G[16 * g : 16 * g + 16, MAIN:] = rest_piece(total[3 * ROWS :, :], g)
        grads = G[...]
        state = state_col[...] + jnp.sum(grads * grads, axis=1, keepdims=True) * (1.0 / WIDTH)
        state_col[...] = state
        E[...] = E[...] - grads * (learning_rate / jnp.sqrt(state))

    emb_out[...] = E[:, :WIDTH]
    state_out[...] = jnp.sum(
        jnp.where(diag, jnp.broadcast_to(state_col[...], (ROWS, ROWS)), 0.0), axis=0, keepdims=True
    )
    drain()


def local(embeddings, adagrad_state, source_rows, target_rows, negative_rows, edge_counts):
    vmem = pl.BlockSpec(memory_space=pltpu.VMEM)
    DMA = pltpu.SemaphoreType.DMA
    table, state = pl.pallas_call(
        kernel,
        name="bucket_rounds",
        out_shape=(
            pltpu.VMEM((ROWS, WIDTH), f32),
            pltpu.VMEM((1, ROWS), f32),
        ),
        in_specs=[pl.BlockSpec(memory_space=pl.ANY)] * 6,
        out_specs=(vmem, vmem),
        scratch_shapes=[
            pltpu.VMEM((ROWS, WIDTH), f32),
            pltpu.VMEM((1, ROWS), f32),
            pltpu.VMEM((ROUNDS, SLOTS), jnp.int32),
            pltpu.VMEM((ROUNDS, SLOTS), jnp.int32),
            pltpu.VMEM((ROUNDS, NEG), jnp.int32),
            pltpu.VMEM((1, ROUNDS), jnp.int32),
            pltpu.VMEM((ROUNDS, 8, SLOTS), jnp.int32),
            pltpu.VMEM((ROWS, LANES), f32),
            pltpu.VMEM((ROWS, LANES), f32),
            pltpu.VMEM((ROWS, 1), f32),
            pltpu.VMEM((8, SLOTS), jnp.int32),
            pltpu.VMEM((ROUNDS, PACKED, 128), bf16),
            pltpu.VMEM((ROUNDS, 16, PACKED, 128), bf16),
            pltpu.VMEM((ROUNDS, 16, PACKED, 128), bf16),
            pltpu.VMEM((ENT, LANES), bf16),
            pltpu.VMEM((ENT, LANES), bf16),
            pltpu.VMEM((4, SLOTS, BLOCK), bf16),
            pltpu.VMEM((ENT, SLOTS), bf16),
            pltpu.VMEM((ENT, 1), f32),
            pltpu.VMEM((ENT, SLOTS), bf16),
            pltpu.VMEM((BLOCK, LANES), f32),
            pltpu.VMEM((ROUNDS, 4, 4, PACKED, 128), bf16),
            pltpu.VMEM((ROUNDS, 4, 4, PACKED, 128), bf16),
            pltpu.VMEM((ROUNDS, 4, PACKED, 128), bf16),
            pltpu.VMEM((ROUNDS, 4, PACKED, 128), bf16),
            pltpu.VMEM((ROUNDS, 2, 4, PACKED, 128), bf16),
            pltpu.VMEM((ROUNDS, 2, 4, PACKED, 128), bf16),
            pltpu.VMEM((3, 4, PACKED, 128), f32),
            pltpu.VMEM((ROUNDS, 4, PACKED, 128), bf16),
            pltpu.VMEM((ROUNDS, 4, PACKED, 128), bf16),
            pltpu.VMEM((SLOTS, LANES), f32),
            pltpu.VMEM((SLOTS, LANES), f32),
            DMA((104,)),
            DMA((ROUNDS, 16)),
            DMA((ROUNDS, 3)),
            DMA((ROUNDS, 4)),
            DMA((ROUNDS, 4)),
            DMA((ROUNDS, 4)),
            DMA((ROUNDS, 2, 4)),
            DMA((ROUNDS, 4)),
            DMA((1,)),
            DMA((6,)),
        ],
        compiler_params=pltpu.CompilerParams(
            collective_id=0, has_side_effects=True, vmem_limit_bytes=56 * 1024 * 1024
        ),
        cost_estimate=pl.CostEstimate(
            flops=2 * ROUNDS * 5 * ENT * SLOTS * WIDTH,
            bytes_accessed=4 * ROWS * WIDTH * 2,
            transcendentals=ROUNDS * ENT * SLOTS,
        ),
    )(
        embeddings,
        adagrad_state.reshape(1, ROWS),
        source_rows,
        target_rows,
        negative_rows,
        edge_counts.reshape(1, ROUNDS),
    )
    return table, state.reshape(ROWS)


def solution(mesh):
    in_specs = (
        P(("dom", "edge"), None),
        P(("dom", "edge")),
        P(None, ("dom", "edge")),
        P(None, ("dom", "edge")),
        P(None, ("dom", "edge")),
        P(None, ("dom", "edge")),
    )
    out_specs = (P(("dom", "edge"), None), P(("dom", "edge")))
    return jax.shard_map(local, mesh=mesh, in_specs=in_specs, out_specs=out_specs, check_vma=False)
```

profile of v0, /device:TPU:1, one launch (start us, length us, event | category | flops | bytes accessed | tf_op | source)
XLA Modules:
  0.0 94.6 jit_solution(10984541654314137201)
XLA Ops:
  0.6 92.7 %bucket_rounds.1 = (f32[96,400]{1,0:T(8,128)S(1)}, f32[1,96]{1,0:T(1,128)S(1)}) custom-call(f32[96,400]{1,0:T(8,128)} %emb_hbm.1, f32[1,96]{1,0:T(1,128)} %bitcast.4, s32[2,512]{1,0:T(2,128)} %source_hbm.1, s32[2,512]{1,0:T(2,128)} %target_hbm.1, s32[2,1000]{1,0:T(2,128)} %negative_hbm.1, s32[1,2]{1,0:T(1,128)} %bitcast.5), custom_call_target="tpu_custom_call" | custom-call | flops 6291456000 | bytes 307200 | tf_op jit(solution)/shard_map/bucket_rounds/pallas_call | solution.py:440
  93.4 0.7 copy.10
  94.1 0.5 copy.11
where the time goes:
time: 94.9 us; the launch traced here: 94.6 us
  Pallas kernels  92.7 us (98%)
  local copies, waits for them, and re-layouts  1.19 us (1%)
    pallas_call x1, Pallas kernels, local(): pl.pallas_call(kernel, name='bucket_rounds', out_shape=(pltpu.VMEM((ROWS,...  92.7 us

commit v1 on v0

--- a/solution.py
+++ b/solution.py
@@ -47,7 +47,7 @@
 
 def kernel(
     emb_hbm, state_hbm, source_hbm, target_hbm, negative_hbm, count_hbm, emb_out, state_out,
-    emb_ref, state_ref, source_ref, target_ref, negative_ref, count_ref, idx_ref, E, G, state_col, idx_far, own_pk, Lo, Lp, To, Tp, hot, HS, cnt, MT, tmp,
+    emb_ref, state_ref, source_ref, target_ref, negative_ref, count_ref, idx_ref, E, G, state_col, idx_far, own_pk, Lo, Lp, To, Tp, hot, HS, Us, Ws, MT, tmp,
     PBs, PBr, OBs, OBr, YBs, YBr, GO, ZBs, ZBr, Sv, Gv,
     ss, r_own, r_par, r_parq, r_pb, r_ob, r_yb, r_zb, r_idx, r_in,
 ):
@@ -168,13 +168,19 @@
 
     def multiplicity(r):
         first, second = row_of(r, 2), row_of(r, 3)
+        target = row_of(r, 1)
+        slot_at = lax.broadcasted_iota(jnp.int32, (1, SLOTS), 1).astype(f32)
+        live = jnp.where(slot_at < row_of(r, 4), 0.5, 0.0)
         row = lax.broadcasted_iota(jnp.int32, (128, SLOTS), 0)
 
         @pl.loop(0, ENT // 128)
         def _(i):
             at = (row + i * 128).astype(f32)
             total = jnp.where(first == at, 1.0, 0.0) + jnp.where(second == at, 1.0, 0.0)
-            cnt[pl.ds(i * 128, 128), :] = jnp.sum(total, axis=1, keepdims=True) * (1.0 / NEG)
+            share = jnp.sum(total, axis=1, keepdims=True) * (1.0 / NEG)
+            same = jnp.where(target == at, 1.0, 0.0)
+            Us[pl.ds(i * 128, 128), :] = live * (share + same)
+            Ws[pl.ds(i * 128, 128), :] = live * (share - same)
 
     def assemble(L, T, r, slot):
         base = slot * ROWS
@@ -305,10 +311,6 @@
             assemble(Lp, Tp, r, slot)
 
         half = (Sv[...] * 0.5).astype(bf16)
-        target = row_of(r, 1)
-        slot_at = lax.broadcasted_iota(jnp.int32, (1, SLOTS), 1).astype(f32)
-        live = jnp.where(slot_at < row_of(r, 4), 0.5, 0.0)
-
         def weights(i, held):
             rows = pl.ds(pl.multiple_of(i * BLOCK, BLOCK), BLOCK)
             t = jnp.tanh(
@@ -316,14 +318,13 @@
                     Tp[rows, :], half, (((1,), (1,)), ((), ())), preferred_element_type=f32
                 )
             )
-            at = (lax.broadcasted_iota(jnp.int32, (BLOCK, SLOTS), 0) + i * BLOCK).astype(f32)
-            same = target == at
-            m = live * (cnt[rows, :] * (1.0 + t) + jnp.where(same, t - 1.0, 0.0))
+            slope, level = Us[rows, :], Ws[rows, :]
+            m = slope * t + level
             weight = m.astype(bf16)
             MT[rows, :] = weight
-            return held + jnp.sum(jnp.where(same, m, 0.0), axis=0, keepdims=True)
-
-        held = lax.fori_loop(0, ENT // BLOCK, weights, jnp.zeros((1, SLOTS), f32))
+            return held + jnp.sum((slope - level) * m, axis=0, keepdims=True)
+
+        held = lax.fori_loop(0, ENT // BLOCK, weights, jnp.zeros((1, SLOTS), f32), unroll=True)
         rounded = held.astype(bf16).astype(f32)
         ratio = jnp.where(rounded == 0.0, 1.0, held / jnp.where(rounded == 0.0, 1.0, rounded))
         ratio = jnp.transpose(jnp.broadcast_to(ratio, (128, SLOTS)))
@@ -465,7 +466,8 @@
             pltpu.VMEM((ENT, LANES), bf16),
             pltpu.VMEM((4, SLOTS, BLOCK), bf16),
             pltpu.VMEM((ENT, SLOTS), bf16),
-            pltpu.VMEM((ENT, 1), f32),
+            pltpu.VMEM((ENT, SLOTS), f32),
+            pltpu.VMEM((ENT, SLOTS), f32),
             pltpu.VMEM((ENT, SLOTS), bf16),
             pltpu.VMEM((BLOCK, LANES), f32),
             pltpu.VMEM((ROUNDS, 4, 4, PACKED, 128), bf16),

time: 94.9 us -> 92.4 us (0.974)
  Pallas kernels: 92.7 us -> 90.5 us
    pallas_call x1, Pallas kernels: 92.7 us -> 90.5 us  [local(): pl.pallas_call(kernel, name='bucket_rounds', out_shape=(pltpu.VMEM((ROWS,...]
where the time goes in v1:
time: 92.4 us; the launch traced here: 92.3 us
  Pallas kernels  90.5 us (98%)
  local copies, waits for them, and re-layouts  1.19 us (1%)
    pallas_call x1, Pallas kernels, local(): pl.pallas_call(kernel, name='bucket_rounds', out_shape=(pltpu.VMEM((ROWS,...  90.5 us

profile of v1, /device:TPU:1, one launch (start us, length us, event | category | flops | bytes accessed | tf_op | source)
XLA Modules:
  0.0 92.3 jit_solution(5768015945506664014)
XLA Ops:
  0.6 90.5 %bucket_rounds.1 = (f32[96,400]{1,0:T(8,128)S(1)}, f32[1,96]{1,0:T(1,128)S(1)}) custom-call(f32[96,400]{1,0:T(8,128)} %emb_hbm.1, f32[1,96]{1,0:T(1,128)} %bitcast.4, s32[2,512]{1,0:T(2,128)} %source_hbm.1, s32[2,512]{1,0:T(2,128)} %target_hbm.1, s32[2,1000]{1,0:T(2,128)} %negative_hbm.1, s32[1,2]{1,0:T(1,128)} %bitcast.5), custom_call_target="tpu_custom_call" | custom-call | flops 6291456000 | bytes 307200 | tf_op jit(solution)/shard_map/bucket_rounds/pallas_call | solution.py:441
  91.1 0.7 copy.10
  91.8 0.5 copy.11

commit v2 on v1

--- a/solution.py
+++ b/solution.py
@@ -209,7 +209,6 @@
 
         if r == 0:
             keep()
-            source_hot(0)
             pl.semaphore_wait(barrier, 6 + 4 * ((zh + c) % 2))
         else:
             pl.when(stay)(keep)
@@ -273,15 +272,18 @@
             def _():
                 idx_far[...] = idx_ref[1]
 
+            source_hot(0)
             multiplicity(0)
         else:
             arrived(idx_far, r_idx.at[0], mover)
             source_hot(1)
         line(1)
+        if r == 1:
+            multiplicity(1)
         line(2)
+        scatter_hot(r)
         line(3)
         sibling_block(y, 0)
-        scatter_hot(r)
         block_wait(ym, 0, up)
         block_wait(yp, 0)
         block_wait(yp, 1, down)
@@ -295,8 +297,6 @@
         opposite(0)
         opposite(1)
         sources(0, y)
-        if r == 1:
-            multiplicity(1)
         sources(1, yp)
         partner(0, y)
         sources(2, ym)
@@ -385,14 +385,14 @@
         own(0, yo)
         send_opposite(3)
         send_opposite(2)
+        send_opposite(1)
+        send_opposite(0)
         peer(1, yp)
         peer(2, ym)
         own(1, yp)
         send_block(0, 3)
         own(2, ym)
         send_block(1, 2)
-        send_opposite(1)
-        send_opposite(0)
         peer(3, y)
         add_opposite(2)
         add_opposite(3)

time: 92.4 us -> 89.9 us (0.973)
  Pallas kernels: 90.5 us -> 88 us
    pallas_call x1, Pallas kernels: 90.5 us -> 88 us  [local(): pl.pallas_call(kernel, name='bucket_rounds', out_shape=(pltpu.VMEM((ROWS,...]
where the time goes in v2:
time: 89.9 us; the launch traced here: 89.8 us
  Pallas kernels  88 us (98%)
  local copies, waits for them, and re-layouts  1.19 us (1%)
    pallas_call x1, Pallas kernels, local(): pl.pallas_call(kernel, name='bucket_rounds', out_shape=(pltpu.VMEM((ROWS,...  88 us

profile of v2, /device:TPU:1, one launch (start us, length us, event | category | flops | bytes accessed | tf_op | source)
XLA Modules:
  0.0 89.8 jit_solution(12217832721214305118)
XLA Ops:
  0.6 88.0 %bucket_rounds.1 = (f32[96,400]{1,0:T(8,128)S(1)}, f32[1,96]{1,0:T(1,128)S(1)}) custom-call(f32[96,400]{1,0:T(8,128)} %emb_hbm.1, f32[1,96]{1,0:T(1,128)} %bitcast.4, s32[2,512]{1,0:T(2,128)} %source_hbm.1, s32[2,512]{1,0:T(2,128)} %target_hbm.1, s32[2,1000]{1,0:T(2,128)} %negative_hbm.1, s32[1,2]{1,0:T(1,128)} %bitcast.5), custom_call_target="tpu_custom_call" | custom-call | flops 6291456000 | bytes 307200 | tf_op jit(solution)/shard_map/bucket_rounds/pallas_call | solution.py:441
  88.6 0.7 copy.10
  89.3 0.5 copy.11

commit v3 on v2

--- a/solution.py
+++ b/solution.py
@@ -121,25 +121,13 @@
     ):
         loads.append(pltpu.make_async_copy(src, dst, r_in.at[i]))
         loads[-1].start()
-    idx_ref[...] = jnp.full((ROUNDS, 8, SLOTS), -1, jnp.int32)
-    for load in loads:
-        load.wait()
-    for r in range(ROUNDS):
-        idx_ref[r, 0:1, :] = source_ref[r : r + 1, :]
-        idx_ref[r, 1:2, :] = target_ref[r : r + 1, :]
-        idx_ref[r, 2:3, :] = negative_ref[r : r + 1, :SLOTS]
-        idx_ref[r, 3:4, : NEG - SLOTS] = negative_ref[r : r + 1, SLOTS:]
-        idx_ref[r, 4:5, :] = jnp.broadcast_to(count_ref[:, r : r + 1], (1, SLOTS))
+    loads[0].wait()
 
     E[:, MAIN:] = jnp.zeros((ROWS, LANES - MAIN), f32)
     E[:, :WIDTH] = emb_ref[...]
     diag = lax.broadcasted_iota(jnp.int32, (ROWS, ROWS), 0) == lax.broadcasted_iota(
         jnp.int32, (ROWS, ROWS), 1
     )
-    state_col[...] = jnp.sum(
-        jnp.where(diag, jnp.broadcast_to(state_ref[...], (ROWS, ROWS)), 0.0), axis=1, keepdims=True
-    )
-
     def pack_own(r):
         for g in range(3):
             own_pk[r, ROWS * g : ROWS * (g + 1), :] = E[:, 128 * g : 128 * (g + 1)].astype(bf16)
@@ -222,19 +210,6 @@
             a, b = flip(z, k), flip(z, 4 - k)
             return a if r == 0 else a + ((zh + c) % 2) * (b - a)
 
-        for k in range(4):
-            if k > 0 or r == 1:
-                send(
-                    own_pk.at[r], Lo.at[r, e], r_own.at[r, e], dev(zt, ct, y, turn(k)),
-                    mover if k == 0 else None,
-                )
-
-        def block_wait(block, k, to=None):
-            slot = block * 4 + turn(k)
-            arrived(Lo.at[r, slot], r_own.at[r, slot])
-            if to is not None:
-                send(Lo.at[r, slot], Lo.at[r, slot], r_own.at[r, slot], to)
-
         def line(k):
             slot = y * 4 + turn(k)
             if k > 0:
@@ -244,6 +219,21 @@
             send(Lo.at[r, slot], Lo.at[r, slot], r_own.at[r, slot], up)
             send(Lo.at[r, slot], Lo.at[r, slot], r_own.at[r, slot], down)
 
+        if r == 0:
+            line(0)
+        for k in range(4):
+            if k > 0 or r == 1:
+                send(
+                    own_pk.at[r], Lo.at[r, e], r_own.at[r, e], dev(zt, ct, y, turn(k)),
+                    mover if k == 0 else None,
+                )
+
+        def block_wait(block, k, to=None):
+            slot = block * 4 + turn(k)
+            arrived(Lo.at[r, slot], r_own.at[r, slot])
+            if to is not None:
+                send(Lo.at[r, slot], Lo.at[r, slot], r_own.at[r, slot], to)
+
         def sibling_block(block, q):
             send(Lo.at[r, pl.ds(block * 4, 4)], Lp.at[r, pl.ds(block * 4, 4)], r_par.at[r, q], sib)
 
@@ -264,8 +254,21 @@
             for k in range(4):
                 assemble(Lp, Tp, r, block * 4 + k)
 
-        line(0)
+        if r == 1:
+            line(0)
         if r == 0:
+            idx_ref[...] = jnp.full((ROUNDS, 8, SLOTS), -1, jnp.int32)
+            for load in loads[1:]:
+                load.wait()
+            for q in range(ROUNDS):
+                idx_ref[q, 0:1, :] = source_ref[q : q + 1, :]
+                idx_ref[q, 1:2, :] = target_ref[q : q + 1, :]
+                idx_ref[q, 2:3, :] = negative_ref[q : q + 1, :SLOTS]
+                idx_ref[q, 3:4, : NEG - SLOTS] = negative_ref[q : q + 1, SLOTS:]
+                idx_ref[q, 4:5, :] = jnp.broadcast_to(count_ref[:, q : q + 1], (1, SLOTS))
+            state_col[...] = jnp.sum(
+                jnp.where(diag, jnp.broadcast_to(state_ref[...], (ROWS, ROWS)), 0.0), axis=1, keepdims=True
+            )
             send(idx_ref.at[1], idx_far, r_idx.at[0], dev(c, zh, y, z), mover)
 
             @pl.when(jnp.logical_not(mover))

time: 89.9 us -> 89.9 us (level)
  no operation moved by 1% of the time
where the time goes in v3:
time: 89.9 us
  Pallas kernels  88 us (98%)
  local copies, waits for them, and re-layouts  1.19 us (1%)
    pallas_call x1, Pallas kernels, local(): pl.pallas_call(kernel, name='bucket_rounds', out_shape=(pltpu.VMEM((ROWS,...  88 us

profile of v3, /device:TPU:1, one launch (start us, length us, event | category | flops | bytes accessed | tf_op | source)
XLA Modules:
  0.0 89.9 jit_solution(13240427657148580435)
XLA Ops:
  0.6 88.0 %bucket_rounds.1 = (f32[96,400]{1,0:T(8,128)S(1)}, f32[1,96]{1,0:T(1,128)S(1)}) custom-call(f32[96,400]{1,0:T(8,128)} %emb_hbm.1, f32[1,96]{1,0:T(1,128)} %bitcast.4, s32[2,512]{1,0:T(2,128)} %source_hbm.1, s32[2,512]{1,0:T(2,128)} %target_hbm.1, s32[2,1000]{1,0:T(2,128)} %negative_hbm.1, s32[1,2]{1,0:T(1,128)} %bitcast.5), custom_call_target="tpu_custom_call" | custom-call | flops 6291456000 | bytes 307200 | tf_op jit(solution)/shard_map/bucket_rounds/pallas_call | solution.py:444
  88.7 0.7 copy.10
  89.3 0.5 copy.11
